TPU v7x, 32 devices: a whole 2x2x4 slice. The times are simulated.
32 devices in a mesh: band: 8 (over z, y), mp: 4 (over x, core).
Axes of the slice: x: 2, y: 2, z: 4, core: 2. Of those that a mesh axis runs over, the one named last changes fastest.
Arguments:
- cells: bfloat16 [2048, 1024], P('band', 'mp'), may hold values from -81 to 81
- row_gain: float32 [1024], replicated, may hold values from 0.1 to 1.9
- row_qkv: bfloat16 [3, 1024, 1024], P(None, None, 'mp'), may hold values from -1.25 to 1.25
- row_out: bfloat16 [1024, 1024], P('mp'), may hold values from -0.1875 to 0.1875
- col_gain: float32 [1024], replicated, may hold values from 0.1 to 1.9
- col_qkv: bfloat16 [3, 1024, 1024], P(None, None, 'mp'), may hold values from -1.25 to 1.25
- col_out: bfloat16 [1024, 1024], P('mp'), may hold values from -0.1875 to 0.1875
- row_seg: int32 [2048], P('band'), may hold values from 0 to 255, never falling along the last dimension, each value on 1 to 16 neighbouring positions
- col_dest: int32 [2048, 1], P('band'), may hold values from 0 to 7; in each aligned block of 256 rows (0 to 255, 256 to 511, ...) at most 48 rows name the same one
- sheet_column_index: int32 [2048], P('band'), may hold values from 1 to 8
- d_result: bfloat16 [2048, 1024], P('band', 'mp'), may hold values from -6 to 6
Outputs:
- result: bfloat16 [2048, 1024], P('band', 'mp')
- d_cells: bfloat16 [2048, 1024], P('band', 'mp')
Inputs may be any that keep to these rules, and one draw needn't show every extreme that they name: `row_seg`: cells never fall in value along the array. `col_dest`: at most 48 of the cells of one row band name the same column band, and some row band sends exactly 48 to some column band.
All inputs are finite; a program needn't handle non-finite values.
Results may differ from a plain program's by a relative error of at most 0.019.
Values may be sent and summed in bfloat16 or wider, within the bound.
A program may use at most 64 MiB of HBM per device.

v0:
```python
import jax
import jax.numpy as jnp
from jax import lax
from jax.sharding import PartitionSpec as P

HEAD_DIM = 64
TILE = 128
norm_eps = 1e-06
neg_fill = -1e30


def block_terms(inputs, norm_gain, query_key_value_weight, w_out, allowed, tile_rows):
    values = inputs.astype(jnp.float32)
    inv_rms = lax.rsqrt(jnp.mean(values * values, axis=-1, keepdims=True) + norm_eps)
    normalized_cells = (values * inv_rms * norm_gain).astype(jnp.bfloat16)
    projected_heads = jnp.einsum(
        "lu,xuh->xlh", normalized_cells, query_key_value_weight, preferred_element_type=jnp.float32
    ).astype(jnp.bfloat16)
    row_count = inputs.shape[0]
    feat_width = query_key_value_weight.shape[2]
    head_count = feat_width // HEAD_DIM
    shaped = projected_heads.reshape(3, row_count // tile_rows, tile_rows, head_count, HEAD_DIM)
    scores = jnp.einsum(
        "bqhe,bkhe->bhqk", shaped[0], shaped[1], preferred_element_type=jnp.float32
    ) * HEAD_DIM ** (-0.5)
    scores = jnp.where(allowed[:, None], scores, neg_fill)
    scores = scores - lax.stop_gradient(jnp.max(scores, axis=-1, keepdims=True))
    expd = jnp.exp(scores)
    attn_probs = (expd / jnp.sum(expd, axis=-1, keepdims=True)).astype(jnp.bfloat16)
    attended = jnp.einsum(
        "bhqk,bkhe->bqhe", attn_probs, shaped[2], preferred_element_type=jnp.float32
    ).astype(jnp.bfloat16)
    attended = attended.reshape(row_count, feat_width)
    return jnp.dot(attended, w_out, preferred_element_type=jnp.float32)


def column_band_mask(col_keys):
    positions = jnp.arange(col_keys.shape[0])
    same_col = (col_keys[:, None] == col_keys[None, :]) & (col_keys[None, :] > 0)
    return (same_col | (positions[:, None] == positions[None, :]))[None]


def widen(block):
    return lax.all_gather(block, "mp", axis=1, tiled=True)


def narrow(terms):
    return lax.psum_scatter(
        terms.astype(jnp.bfloat16), "mp", scatter_dimension=1, tiled=True
    ).astype(jnp.float32)


def move_rows(rows):
    return lax.all_to_all(rows, "band", split_axis=0, concat_axis=0, tiled=True)


def on_device(
    cells,
    row_gain,
    row_qkv,
    row_out,
    col_gain,
    col_qkv,
    col_out,
    row_seg,
    col_dest,
    sheet_column_index,
    d_result,
):
    cell_rows, feat_width = cells.shape
    band_count = lax.axis_size("band")
    capacity = max(2, 3 * cell_rows // (2 * band_count))
    slot_total = band_count * capacity
    gathered = widen(cells)
    row_groups = row_seg.reshape(cell_rows // TILE, TILE)
    row_mask = row_groups[:, :, None] == row_groups[:, None, :]

    def row_local(inputs):
        return block_terms(inputs, row_gain, row_qkv, row_out, row_mask, TILE)

    row_terms, row_pull = jax.vjp(row_local, gathered)
    target = col_dest[:, 0]
    place = jnp.arange(cell_rows, dtype=jnp.int32)
    earlier = (target[:, None] == target[None, :]) & (place[None, :] < place[:, None])
    ranking = jnp.sum(earlier.astype(jnp.int32), axis=1)
    slot_index = target * capacity + ranking
    keys_out = (
        jnp.zeros((slot_total,), jnp.bfloat16)
        .at[slot_index]
        .set(sheet_column_index.astype(jnp.bfloat16))
    )
    back_in = jnp.zeros((slot_total, feat_width), jnp.bfloat16).at[slot_index].set(d_result)
    mixed_rows = (cells.astype(jnp.float32) + narrow(row_terms)).astype(jnp.bfloat16)
    outgoing = jnp.zeros((slot_total, feat_width), jnp.bfloat16).at[slot_index].set(mixed_rows)
    arrived, col_keys = (
        lax.all_to_all(outgoing, "band", split_axis=0, concat_axis=0, tiled=True),
        lax.all_to_all(keys_out, "band", split_axis=0, concat_axis=0, tiled=True),
    )
    column_full = widen(arrived)
    col_allowed = column_band_mask(col_keys)

    def col_local(inputs):
        return block_terms(inputs, col_gain, col_qkv, col_out, col_allowed, inputs.shape[0])

    col_terms, col_pull = jax.vjp(col_local, column_full)
    settled = (arrived.astype(jnp.float32) + narrow(col_terms)).astype(jnp.bfloat16)
    result = move_rows(settled)[slot_index]
    d_column = move_rows(back_in)
    (d_col_part,) = col_pull(widen(d_column).astype(jnp.float32))
    d_mixed_col = (d_column.astype(jnp.float32) + narrow(d_col_part.astype(jnp.float32))).astype(
        jnp.bfloat16
    )
    d_mixed = move_rows(d_mixed_col)[slot_index]
    (d_row_part,) = row_pull(widen(d_mixed).astype(jnp.float32))
    d_cells = (d_mixed.astype(jnp.float32) + narrow(d_row_part.astype(jnp.float32))).astype(
        jnp.bfloat16
    )
    return (result, d_cells)


def solution(mesh):
    in_specs = (
        P("band", "mp"),
        P(),
        P(None, None, "mp"),
        P("mp", None),
        P(),
        P(None, None, "mp"),
        P("mp", None),
        P("band"),
        P("band", None),
        P("band"),
        P("band", "mp"),
    )
    out_specs = (P("band", "mp"), P("band", "mp"))
    return jax.shard_map(
        on_device, mesh=mesh, in_specs=in_specs, out_specs=out_specs, check_vma=False
    )
```

profile of v0, /device:TPU:0, one launch (start us, length us, event | category | flops | bytes accessed | tf_op | source)
XLA Modules:
  0.0 187.2 jit_solution(12250987462010092255)
XLA Ops:
  7.2 9.0 %all_gather.12 = bf16[256,1024]{1,0:T(8,128)(2,1)S(1)} all-gather(bf16[256,256]{1,0:T(8,128)(2,1)} %param.11), channel_id=1, replica_groups=mesh['band'=8,'mp'=4] {'mp'}, dimensions={1}, use_global_device_ids=true | all-gather | bytes 655360 | tf_op jit(solution)/shard_map/all_gather | solution.py:44
  16.2 0.2 fusion.34
  16.4 2.1 %fusion.21 = bf16[3,256,256]{2,1,0:T(8,128)(2,1)S(1)} fusion(bf16[3,1024,256]{2,1,0:T(8,128)(2,1)} %param.13, bf16[256,1024]{1,0:T(8,128)(2,1)S(1)} %all_gather.12, f32[1024]{0:T(1024)} %param.12, f32[256]{0:T(256)S(1)} %fusion.61), kind=kOutput, calls=%fused_computation.50 | convolution fusion | flops 403898368 | bytes 2495488 | tf_op jit(solution)/shard_map/jvp(lu,xuh->xlh)/dot_general | solution.py:16
  18.5 0.2 reshape.309
  18.7 0.2 copy.84
  18.8 0.2 reshape.310
  19.0 0.2 copy.85
  19.2 0.1 broadcast_compare_fusion
  19.3 0.2 reshape.308
  19.5 0.2 copy.86
  19.7 1.2 fusion.73
  20.9 1.3 fusion.29
  22.2 0.1 copy.88
  22.3 1.1 convolution_convert_fusion.3
  23.5 0.2 convert_reduce_fusion
  23.7 2.2 %scatter_custom_fusion.1 = bf16[384]{0:T(512)(128)(2,1)S(1)} fusion(s32[256]{0:T(256)S(1)} %bitcast.155, bf16[256]{0:T(256)(128)(2,1)S(1)} %convert_element_type.204, bf16[]{:T(256)} %constant.12.clone.1), kind=kCustom, calls=%fused_computation.121 | custom fusion | bytes 770 | tf_op jit(solution)/shard_map/scatter | solution.py:90
  25.9 0.7 all_to_all.52
  26.5 5.8 %all-to-all-start.1 = ((bf16[8,48,1]{1,2,0:T(2,128)(2,1)}), bf16[8,48,1]{1,2,0:T(2,128)(2,1)S(1)}, u32[]{:S(2)}, u32[]{:S(2)}) async-start(bf16[8,48,1]{1,2,0:T(2,128)(2,1)} %all_to_all.52), calls=%async_computation.2 | async-start | bytes 8192 | tf_op jit(solution)/shard_map/all_to_all | solution.py:97
  32.4 2.5 %scatter_custom_fusion.2 = bf16[384,256]{1,0:T(8,128)(2,1)} fusion(s32[256]{0:T(256)S(1)} %bitcast.156, bf16[256,256]{1,0:T(8,128)(2,1)} %param.21, bf16[]{:T(256)} %constant.12.clone.1), kind=kCustom, calls=%fused_computation.106 | custom fusion | bytes 197120 | tf_op jit(solution)/shard_map/scatter | solution.py:92
  34.8 4.0 %all-to-all-done.1 = bf16[8,48,1]{1,2,0:T(2,128)(2,1)S(1)} async-done(((bf16[8,48,1]{1,2,0:T(2,128)(2,1)}), bf16[8,48,1]{1,2,0:T(2,128)(2,1)S(1)}, u32[]{:S(2)}, u32[]{:S(2)}) %all-to-all-start.1) | async-done | bytes 800 | tf_op jit(solution)/shard_map/all_to_all | solution.py:97
  38.8 3.4 %all-to-all-start.3 = ((bf16[8,48,256]{2,1,0:T(8,128)(2,1)}), bf16[8,48,256]{2,1,0:T(8,128)(2,1)S(1)}, u32[]{:S(2)}, u32[]{:S(2)}) async-start(bf16[8,48,256]{2,1,0:T(8,128)(2,1)} %bitcast.19), calls=%async_computation.5 | async-start | bytes 393216 | tf_op jit(solution)/shard_map/all_to_all | solution.py:54
  42.4 0.8 fusion.43
  43.2 2.9 %reduce-scatter.5.cloned.1.call-done = bf16[256,256]{1,0:T(8,128)(2,1)} async-done(((bf16[256,1024]{1,0:T(8,128)(2,1)}), bf16[256,256]{1,0:T(8,128)(2,1)}) %reduce-scatter.5.cloned.1.call-update) | async-done | bytes 131088 | tf_op jit(solution)/shard_map/reduce_scatter | solution.py:48
  46.1 2.5 %scatter_custom_fusion = bf16[384,256]{1,0:T(8,128)(2,1)} fusion(s32[256]{0:T(256)S(1)} %bitcast.157, bf16[256,256]{1,0:T(8,128)(2,1)} %reduce-scatter.5.cloned.1.call-done, bf16[256,256]{1,0:T(8,128)(2,1)S(1)} %copy-done.12, bf16[]{:T(256)} %constant.12.clone.1), kind=kCustom, calls=%fused_computation.101 | custom fusion | flops 262144 | bytes 458754 | tf_op jit(solution)/shard_map/scatter | solution.py:94
  48.6 1.3 all-to-all-done.3
  50.0 4.3 %all-to-all-start = ((bf16[8,48,256]{2,1,0:T(8,128)(2,1)}), bf16[8,48,256]{2,1,0:T(8,128)(2,1)S(1)}, u32[]{:S(2)}, u32[]{:S(2)}) async-start(bf16[8,48,256]{2,1,0:T(8,128)(2,1)} %bitcast.7), calls=%async_computation.1 | async-start | bytes 393216 | tf_op jit(solution)/shard_map/all_to_all | solution.py:96
  54.3 7.9 %all_gather.14 = bf16[384,1024]{1,0:T(8,128)(2,1)S(1)} all-gather(bf16[384,256]{1,0:T(8,128)(2,1)S(1)} %bitcast.137), channel_id=1, replica_groups=mesh['band'=8,'mp'=4] {'mp'}, dimensions={1}, use_global_device_ids=true | all-gather | bytes 983040 | tf_op jit(solution)/shard_map/all_gather | solution.py:44
  62.2 0.5 convolution_convert_fusion.9
  62.7 8.9 %all_gather.13 = bf16[384,1024]{1,0:T(8,128)(2,1)S(1)} all-gather(bf16[384,256]{1,0:T(8,128)(2,1)S(1)} %bitcast.136), channel_id=1, replica_groups=mesh['band'=8,'mp'=4] {'mp'}, dimensions={1}, use_global_device_ids=true | all-gather | bytes 983040 | tf_op jit(solution)/shard_map/all_gather | solution.py:44
  71.6 0.2 fusion.10
  71.9 1.1 fusion.18
  73.0 0.8 fusion.71
  73.8 3.5 %fusion.74 = (f32[4,384]{1,0:T(4,128)S(1)}, f32[4,384,384]{1,2,0:T(8,128)}) fusion(pred[384,384]{0,1:T(8,128)(4,1)} %fusion.43, bf16[384,4,64]{0,2,1:T(8,128)(2,1)} %bitcast.150, bf16[384,4,64]{0,2,1:T(8,128)(2,1)} %bitcast.147), kind=kOutput, calls=%fused_computation.131 | convolution fusion | flops 77857152 | bytes 2906112 | tf_op jit(solution)/shard_map/jvp()/sub | solution.py:27
  77.4 3.7 %fusion.7 = (f32[4,384]{1,0:T(4,128)S(1)}, bf16[4,384,384]{1,2,0:T(8,128)(2,1)}, bf16[4,384,384]{1,2,0:T(8,128)(2,1)}) fusion(f32[4,384,384]{1,2,0:T(8,128)} %get-tuple-element.13, f32[4,384]{1,0:T(4,128)S(1)} %multiply_divide_fusion, f32[4,384]{1,0:T(4,128)S(1)} %get-tuple-element.12, bf16[4,64,384]{2,1,0:T(8,128)(2,1)S(1)} %bitcast.141, ...), kind=kOutput, calls=%fused_computation.19 | convolution fusion | flops 79624704 | bytes 5130240 | tf_op jit(solution)/shard_map/transpose(jvp(bhqk,bkhe->bqhe))/dot_general | solution.py:30
  81.1 3.9 %fusion.26 = bf16[1,1,384,4,64]{2,4,3,1,0:T(8,128)(2,1)} fusion(bf16[384,4,64]{0,2,1:T(8,128)(2,1)} %bitcast.151, bf16[4,384,384]{1,2,0:T(8,128)(2,1)} %get-tuple-element.14, f32[4,384]{1,0:T(4,128)S(1)} %neg.13, f32[4,384]{1,0:T(4,128)S(1)} %get-tuple-element.12, pred[384,384]{0,1:T(8,128)(4,1)} %fusion.43, bf16[384,4,64]{0,2,1:T(8,128)(2,1)S(1)} %bitcast.148), kind=kOutput, calls=%fused_computation.61 | convolution fusion | flops 156403584 | bytes 1929216 | tf_op jit(solution)/shard_map/transpose(jvp(bqhe,bkhe->bhqk))/dot_general | solution.py:23
  85.0 3.6 %fusion.27 = bf16[1,1,384,4,64]{2,4,3,1,0:T(8,128)(2,1)} fusion(bf16[384,4,64]{0,2,1:T(8,128)(2,1)S(1)} %bitcast.149, bf16[4,384,384]{1,2,0:T(8,128)(2,1)} %get-tuple-element.14, f32[4,384]{1,0:T(4,128)S(1)} %neg.13, f32[4,384]{1,0:T(4,128)S(1)} %get-tuple-element.12, pred[384,384]{0,1:T(8,128)(4,1)} %fusion.43, bf16[384,4,64]{0,2,1:T(8,128)(2,1)S(1)} %bitcast.152), kind=kOutput, calls=%fused_computation.62 | convolution fusion | flops 156403584 | bytes 1929216 | tf_op jit(solution)/shard_map/transpose(jvp(bqhe,bkhe->bhqk))/dot_general | solution.py:23
  88.7 1.8 fusion.28
  90.5 1.1 pad_add_fusion
  91.6 1.1 copy.95
  92.7 2.0 %fusion.13 = (f32[384]{0:T(512)S(1)}, bf16[384,1024]{1,0:T(8,128)(2,1)S(1)}) fusion(bf16[384,1024]{1,0:T(8,128)(2,1)S(1)} %all_gather.13, f32[1024]{0:T(1024)S(1)} %copy-done.20, bf16[3,1024,256]{2,1,0:T(8,128)(2,1)S(1)} %copy-done, bf16[3,384,256]{2,1,0:T(8,128)(2,1)} %copy.95), kind=kOutput, calls=%fused_computation.32 | convolution fusion | flops 606338688 | bytes 3741184 | tf_op jit(solution)/shard_map/transpose(jvp(lu,xuh->xlh))/dot_general | solution.py:16
  94.7 1.3 fusion.9
  96.0 24.5 %reduce-scatter.9.cloned.1.call-done = bf16[384,256]{1,0:T(8,128)(2,1)} async-done(((bf16[384,1024]{1,0:T(8,128)(2,1)}), bf16[384,256]{1,0:T(8,128)(2,1)}) %reduce-scatter.9.cloned.1.call-update) | async-done | bytes 196624 | tf_op jit(solution)/shard_map/reduce_scatter | solution.py:48
  120.5 1.7 add_convert_fusion
  122.2 5.5 %all-to-all-start.4 = ((bf16[8,48,256]{2,1,0:T(8,128)(2,1)}), bf16[8,48,256]{2,1,0:T(8,128)(2,1)S(1)}, u32[]{:S(2)}, u32[]{:S(2)}) async-start(bf16[8,48,256]{2,1,0:T(8,128)(2,1)} %bitcast.38), calls=%async_computation.7 | async-start | bytes 393216 | tf_op jit(solution)/shard_map/all_to_all | solution.py:54
  127.8 1.7 convolution_convert_fusion.10
  129.5 1.3 convolution_convert_fusion.1
  130.9 4.8 %all-to-all-done.4 = bf16[8,48,256]{2,1,0:T(8,128)(2,1)S(1)} async-done(((bf16[8,48,256]{2,1,0:T(8,128)(2,1)}), bf16[8,48,256]{2,1,0:T(8,128)(2,1)S(1)}, u32[]{:S(2)}, u32[]{:S(2)}) %all-to-all-start.4) | async-done | bytes 196640 | tf_op jit(solution)/shard_map/all_to_all | solution.py:54
  135.7 1.2 gather_fusion.1
  136.9 6.7 %all-gather = bf16[256,1024]{1,0:T(8,128)(2,1)S(1)} all-gather(bf16[256,256]{1,0:T(8,128)(2,1)S(1)} %gather_fusion.1), channel_id=2, replica_groups=mesh['band'=8,'mp'=4] {'mp'}, dimensions={1}, use_global_device_ids=true | all-gather | bytes 655360 | tf_op jit(solution)/shard_map/all_gather | solution.py:44
  143.6 0.3 convolution_convert_fusion.14
  144.1 1.3 multiply_reduce_fusion
  145.5 1.4 fusion.30
  146.9 0.2 fusion.32
  147.1 0.3 fusion.31
  147.5 0.4 copy.105
  147.9 0.3 reshape.262
  148.2 2.2 %fusion.37 = (f32[256]{0:T(256)S(1)}, f32[256,1024]{1,0:T(8,128)S(1)}) fusion(bf16[256,1024]{1,0:T(8,128)(2,1)S(1)} %all_gather.12, f32[1024]{0:T(1024)S(1)} %copy-done.21, bf16[3,1024,256]{2,1,0:T(8,128)(2,1)} %param.13, bf16[3,256,256]{1,2,0:T(8,128)(2,1)S(1)} %reshape.262), kind=kOutput, calls=%fused_computation.77 | convolution fusion | flops 404225792 | bytes 3544064 | tf_op jit(solution)/shard_map/transpose(jvp(lu,xuh->xlh))/dot_general | solution.py:16
  150.3 1.1 fusion.33
  151.4 3.5 %reduce-scatter.7.cloned.1.call-done = bf16[384,256]{1,0:T(8,128)(2,1)} async-done(((bf16[384,1024]{1,0:T(8,128)(2,1)}), bf16[384,256]{1,0:T(8,128)(2,1)}) %reduce-scatter.7.cloned.1.call-update) | async-done | bytes 196624 | tf_op jit(solution)/shard_map/reduce_scatter | solution.py:48
  154.9 1.0 add_convert_fusion.1
  155.9 13.2 %all_to_all.58 = bf16[8,48,256]{2,1,0:T(8,128)(2,1)S(1)} all-to-all(bf16[8,48,256]{2,1,0:T(8,128)(2,1)S(1)} %bitcast.140), channel_id=1, replica_groups=mesh['band'=8,'mp'=4] {'band'}, dimensions={0} | all-to-all | bytes 393216 | tf_op jit(solution)/shard_map/all_to_all | solution.py:54
  169.1 1.8 gather_fusion
  171.0 8.2 %reduce-scatter.11.cloned.1.call-done = bf16[256,256]{1,0:T(8,128)(2,1)} async-done(((bf16[256,1024]{1,0:T(8,128)(2,1)}), bf16[256,256]{1,0:T(8,128)(2,1)}) %reduce-scatter.11.cloned.1.call-update) | async-done | bytes 131088 | tf_op jit(solution)/shard_map/reduce_scatter | solution.py:48
  179.1 1.6 add_convert_fusion.2
  (75 shorter events, 0.8 us)
Async XLA Ops:
  7.2 64.7 %copy-start = (bf16[3,1024,256]{2,1,0:T(8,128)(2,1)S(1)}, bf16[3,1024,256]{2,1,0:T(8,128)(2,1)}, u32[]{:S(2)}) copy-start(bf16[3,1024,256]{2,1,0:T(8,128)(2,1)} %param.16) | copy-start | bytes 4718596
  7.2 39.0 %reduce-scatter.5.cloned.1.call-start = ((), (), s32[]{:S(2)}) async-start(), calls=%async_computation.9 | async-start | bytes 655360 | tf_op jit(solution)/shard_map/reduce_scatter | solution.py:48
  16.4 2.8 %copy-start.22 = (s32[256]{0:T(256)S(1)}, s32[256]{0:T(256)}, u32[]{:S(2)}) copy-start(s32[256]{0:T(256)} %param.18) | copy-start | bytes 3076
  18.8 0.8 copy-start.15
  19.0 3.3 %copy-start.3 = (bf16[256,1024]{1,0:T(8,128)(2,1)S(1)}, bf16[256,1024]{1,0:T(8,128)(2,1)}, u32[]{:S(2)}) copy-start(bf16[256,1024]{1,0:T(8,128)(2,1)} %param.14) | copy-start | bytes 1572868
  19.2 1.7 copy-start.17
  19.6 1.2 copy-start.9
  19.6 3.8 %copy-start.23 = (s32[256]{0:T(256)S(1)}, s32[256]{0:T(256)}, u32[]{:S(2)}) copy-start(s32[256]{0:T(256)} %param.20) | copy-start | bytes 3076
  19.7 3.8 %copy-start.19 = (s32[256,1]{0,1:T(1,128)S(1)}, s32[256,1]{0,1:T(1,128)}, u32[]{:S(2)}) copy-start(s32[256,1]{0,1:T(1,128)} %param.19) | copy-start | bytes 3076
  20.9 25.3 %copy-start.12 = (bf16[256,256]{1,0:T(8,128)(2,1)S(1)}, bf16[256,256]{1,0:T(8,128)(2,1)}, u32[]{:S(2)}) copy-start(bf16[256,256]{1,0:T(8,128)(2,1)} %param.11) | copy-start | bytes 393220
  22.2 40.1 %copy-start.1 = (bf16[256,1024]{1,0:T(8,128)(2,1)S(1)}, bf16[256,1024]{1,0:T(8,128)(2,1)}, u32[]{:S(2)}) copy-start(bf16[256,1024]{1,0:T(8,128)(2,1)} %param.17) | copy-start | bytes 1572868
  26.5 12.3 %all-to-all-start.1 = ((bf16[8,48,1]{1,2,0:T(2,128)(2,1)}), bf16[8,48,1]{1,2,0:T(2,128)(2,1)S(1)}, u32[]{:S(2)}, u32[]{:S(2)}) async-start(bf16[8,48,1]{1,2,0:T(2,128)(2,1)} %all_to_all.52), calls=%async_computation.2 | async-start | bytes 8192 | tf_op jit(solution)/shard_map/all_to_all | solution.py:97
  38.8 11.1 %all-to-all-start.3 = ((bf16[8,48,256]{2,1,0:T(8,128)(2,1)}), bf16[8,48,256]{2,1,0:T(8,128)(2,1)S(1)}, u32[]{:S(2)}, u32[]{:S(2)}) async-start(bf16[8,48,256]{2,1,0:T(8,128)(2,1)} %bitcast.19), calls=%async_computation.5 | async-start | bytes 393216 | tf_op jit(solution)/shard_map/all_to_all | solution.py:54
  48.6 23.3 %copy-start.20 = (f32[1024]{0:T(1024)S(1)}, f32[1024]{0:T(1024)}, u32[]{:S(2)}) copy-start(f32[1024]{0:T(1024)} %param.15) | copy-start | bytes 12292
  50.0 12.8 %copy-start.7 = (bf16[8,48,256]{2,1,0:T(8,128)(2,1)}, bf16[8,48,256]{2,1,0:T(8,128)(2,1)S(1)}, u32[]{:S(2)}) copy-start(bf16[8,48,256]{2,1,0:T(8,128)(2,1)S(1)} %all-to-all-done.3) | copy-start | bytes 589828
  50.0 12.7 %all-to-all-start = ((bf16[8,48,256]{2,1,0:T(8,128)(2,1)}), bf16[8,48,256]{2,1,0:T(8,128)(2,1)S(1)}, u32[]{:S(2)}, u32[]{:S(2)}) async-start(bf16[8,48,256]{2,1,0:T(8,128)(2,1)} %bitcast.7), calls=%async_computation.1 | async-start | bytes 393216 | tf_op jit(solution)/shard_map/all_to_all | solution.py:96
  54.3 66.2 %reduce-scatter.9.cloned.1.call-start = ((), (), s32[]{:S(2)}) async-start(), calls=%async_computation.11 | async-start | bytes 983040 | tf_op jit(solution)/shard_map/reduce_scatter | solution.py:48
  62.7 10.3 %copy-start.5 = (bf16[8,48,256]{2,1,0:T(8,128)(2,1)}, bf16[8,48,256]{2,1,0:T(8,128)(2,1)S(1)}, u32[]{:S(2)}) copy-start(bf16[8,48,256]{2,1,0:T(8,128)(2,1)S(1)} %all-to-all-done) | copy-start | bytes 589828
  73.8 7.3 %copy-start.8 = (bf16[1,384,256]{1,2,0:T(8,128)(2,1)}, bf16[1,384,256]{1,2,0:T(8,128)(2,1)S(1)}, u32[]{:S(2)}) copy-start(bf16[1,384,256]{1,2,0:T(8,128)(2,1)S(1)} %get-tuple-element.6) | copy-start | bytes 589828
  77.4 3.7 %copy-start.13 = (bf16[1,384,256]{1,2,0:T(8,128)(2,1)S(1)}, bf16[1,384,256]{1,2,0:T(8,128)(2,1)}, u32[]{:S(2)}) copy-start(bf16[1,384,256]{1,2,0:T(8,128)(2,1)} %get-tuple-element.4) | copy-start | bytes 589828
  81.1 3.9 %copy-start.14 = (bf16[1,384,256]{1,2,0:T(8,128)(2,1)S(1)}, bf16[1,384,256]{1,2,0:T(8,128)(2,1)}, u32[]{:S(2)}) copy-start(bf16[1,384,256]{1,2,0:T(8,128)(2,1)} %get-tuple-element.5) | copy-start | bytes 589828
  94.7 34.9 %copy-start.2 = (bf16[256,1024]{1,0:T(8,128)(2,1)S(1)}, bf16[256,1024]{1,0:T(8,128)(2,1)}, u32[]{:S(2)}) copy-start(bf16[256,1024]{1,0:T(8,128)(2,1)} %param.17) | copy-start | bytes 1572868
  122.2 13.5 %all-to-all-start.4 = ((bf16[8,48,256]{2,1,0:T(8,128)(2,1)}), bf16[8,48,256]{2,1,0:T(8,128)(2,1)S(1)}, u32[]{:S(2)}, u32[]{:S(2)}) async-start(bf16[8,48,256]{2,1,0:T(8,128)(2,1)} %bitcast.38), calls=%async_computation.7 | async-start | bytes 393216 | tf_op jit(solution)/shard_map/all_to_all | solution.py:54
  127.8 27.2 %reduce-scatter.7.cloned.1.call-start = ((), (), s32[]{:S(2)}) async-start(), calls=%async_computation.10 | async-start | bytes 983040 | tf_op jit(solution)/shard_map/reduce_scatter | solution.py:48
  129.5 14.1 %copy-start.4 = (bf16[256,1024]{1,0:T(8,128)(2,1)S(1)}, bf16[256,1024]{1,0:T(8,128)(2,1)}, u32[]{:S(2)}) copy-start(bf16[256,1024]{1,0:T(8,128)(2,1)} %param.14) | copy-start | bytes 1572868
  130.8 13.3 %copy-start.10 = (bf16[2,128,4,64]{1,3,2,0:T(8,128)(2,1)S(1)}, bf16[2,128,4,64]{1,3,2,0:T(8,128)(2,1)}, u32[]{:S(2)}) copy-start(bf16[2,128,4,64]{1,3,2,0:T(8,128)(2,1)} %copy-done.9) | copy-start | bytes 393220
  130.8 48.3 %reduce-scatter.11.cloned.1.call-start = ((), (), s32[]{:S(2)}) async-start(), calls=%async_computation.12 | async-start | bytes 655360 | tf_op jit(solution)/shard_map/reduce_scatter | solution.py:48
  143.6 3.2 %copy-start.18 = (bf16[2,128,4,64]{1,3,2,0:T(8,128)(2,1)S(1)}, bf16[2,128,4,64]{1,3,2,0:T(8,128)(2,1)}, u32[]{:S(2)}) copy-start(bf16[2,128,4,64]{1,3,2,0:T(8,128)(2,1)} %copy-done.17) | copy-start | bytes 393220
  143.9 2.9 %copy-start.11 = (f32[2,4,128,128]{2,3,1,0:T(8,128)S(1)}, f32[2,4,128,128]{2,3,1,0:T(8,128)}, u32[]{:S(2)}) copy-start(f32[2,4,128,128]{2,3,1,0:T(8,128)} %get-tuple-element.11) | copy-start | bytes 1572868
  145.4 1.7 copy-start.16
  147.1 1.0 copy-start.21
  148.2 6.8 %copy-start.6 = (bf16[8,48,256]{2,1,0:T(8,128)(2,1)S(1)}, bf16[8,48,256]{2,1,0:T(8,128)(2,1)}, u32[]{:S(2)}) copy-start(bf16[8,48,256]{2,1,0:T(8,128)(2,1)} %copy-done.5) | copy-start | bytes 589828
Sparse Core Ops, SparseCore 0:
  23.6 22.5 reduce-scatter.4
  96.1 24.3 reduce-scatter.8
  131.1 23.7 reduce-scatter.6
  157.4 21.6 reduce-scatter.10
where the time goes:
time: 188 us; the launch traced here: 187 us
  waiting for transfers between devices  49.3 us (26%)
  blocking collectives  45.7 us (24%)
  matrix products  34.5 us (18%)
  starting transfers between devices  19.2 us (10%)
  between operations  14.3 us (8%)
  local copies, waits for them, and re-layouts  12.3 us (7%)
  other arithmetic  11.9 us (6%)
    reduce_scatter x4, waiting for transfers between devices, narrow(): lax.psum_scatter(terms.astype(jnp.bfloat16), 'mp', scatter_dimension=1, t...  39.1 us
    all_gather x4, blocking collectives, widen(): return lax.all_gather(block, 'mp', axis=1, tiled=True)  32.5 us
    all_to_all x1, blocking collectives, move_rows(): return lax.all_to_all(rows, 'band', split_axis=0, concat_axis=0, tiled=True)  13.2 us
    dot_general x6, matrix products, block_terms(): jnp.einsum('bhqk,bkhe->bqhe', attn_probs, shaped[2], preferred_element_ty...  11.2 us
    all_to_all x2, starting transfers between devices, move_rows(): return lax.all_to_all(rows, 'band', split_axis=0, concat_axis=0, tiled=True)  8.92 us
    dot_general x4, matrix products, block_terms(): jnp.einsum('bqhe,bkhe->bhqk', shaped[0], shaped[1], preferred_element_typ...  8.12 us
    dot_general x4, matrix products, block_terms(): jnp.einsum('lu,xuh->xlh', normalized_cells, query_key_value_weight, prefe...  7.29 us
    all_to_all x2, waiting for transfers between devices, move_rows(): return lax.all_to_all(rows, 'band', split_axis=0, concat_axis=0, tiled=True)  6.16 us
  transfers between devices with their start and end apart: 8, of which 7 were waited for; matrix products, arithmetic and copies ran while one was open for 12% of the time, Pallas kernels for 0%

commit v1 on v0

--- a/solution.py
+++ b/solution.py
@@ -7,6 +7,22 @@
 TILE = 128
 norm_eps = 1e-06
 neg_fill = -1e30
+
+
+def swapped_with_each(array, axis, split, join):
+    ways, here = (lax.axis_size(axis), lax.axis_index(axis))
+    width = array.shape[split] // ways
+    lengths = list(array.shape)
+    lengths[split] = width
+    height = lengths[join]
+    lengths[join] = height * ways
+    full = jnp.zeros(lengths, array.dtype)
+    for mask in range(ways):
+        part = lax.dynamic_slice_in_dim(array, (here ^ mask) * width, width, axis=split)
+        if mask:
+            part = lax.ppermute(part, axis, [(d, d ^ mask) for d in range(ways)])
+        full = lax.dynamic_update_slice_in_dim(full, part, (here ^ mask) * height, axis=join)
+    return full
 
 
 def block_terms(inputs, norm_gain, query_key_value_weight, w_out, allowed, tile_rows):
@@ -93,7 +109,7 @@
     mixed_rows = (cells.astype(jnp.float32) + narrow(row_terms)).astype(jnp.bfloat16)
     outgoing = jnp.zeros((slot_total, feat_width), jnp.bfloat16).at[slot_index].set(mixed_rows)
     arrived, col_keys = (
-        lax.all_to_all(outgoing, "band", split_axis=0, concat_axis=0, tiled=True),
+        swapped_with_each(outgoing, "band", 0, 0),
         lax.all_to_all(keys_out, "band", split_axis=0, concat_axis=0, tiled=True),
     )
     column_full = widen(arrived)

time: 188 us -> 203 us (1.080)
  starting transfers between devices: 19.2 us -> 26.1 us
  waiting for transfers between devices: 49.3 us -> 53.3 us
  local copies, waits for them, and re-layouts: 12.3 us -> 15.1 us
    ppermute x0 -> x7, starting transfers between devices: none -> 11.2 us  [swapped_with_each(): part = lax.ppermute(part, axis, [(d, d ^ mask) for d in range(ways)])]
    all_to_all x2, waiting for transfers between devices: 6.16 us -> 11.5 us  [move_rows(): return lax.all_to_all(rows, 'band', split_axis=0, concat_axis=0, tiled=True)]
    reduce_scatter x4, waiting for transfers between devices: 39.1 us -> 34.7 us  [narrow(): lax.psum_scatter(terms.astype(jnp.bfloat16), 'mp', scatter_dimension=1, t...]
    all_to_all x1 -> x0, starting transfers between devices: 4.31 us -> none  [on_device(): lax.all_to_all(outgoing, 'band', split_axis=0, concat_axis=0, tiled=True)]
    ppermute x0 -> x7, waiting for transfers between devices: none -> 3.11 us  [swapped_with_each(): part = lax.ppermute(part, axis, [(d, d ^ mask) for d in range(ways)])]
  transfers between devices with their start and end apart: 8 -> 14, of which waited for: 7 -> 8; matrix products, arithmetic and copies ran while one was open for 12% -> 11% of each run, Pallas kernels for 0% -> 0%
where the time goes in v1:
time: 203 us; the launch traced here: 202 us
  waiting for transfers between devices  53.3 us (26%)
  blocking collectives  45.6 us (22%)
  matrix products  35.1 us (17%)
  starting transfers between devices  26.1 us (13%)
  local copies, waits for them, and re-layouts  15.1 us (7%)
  between operations  14.3 us (7%)
  other arithmetic  12 us (6%)
    reduce_scatter x4, waiting for transfers between devices, narrow(): lax.psum_scatter(terms.astype(jnp.bfloat16), 'mp', scatter_dimension=1, t...  34.7 us
    all_gather x4, blocking collectives, widen(): return lax.all_gather(block, 'mp', axis=1, tiled=True)  32.3 us
    all_to_all x1, blocking collectives, move_rows(): return lax.all_to_all(rows, 'band', split_axis=0, concat_axis=0, tiled=True)  13.3 us
    all_to_all x2, waiting for transfers between devices, move_rows(): return lax.all_to_all(rows, 'band', split_axis=0, concat_axis=0, tiled=True)  11.5 us
    ppermute x7, starting transfers between devices, swapped_with_each(): part = lax.ppermute(part, axis, [(d, d ^ mask) for d in range(ways)])  11.2 us
    dot_general x6, matrix products, block_terms(): jnp.einsum('bhqk,bkhe->bqhe', attn_probs, shaped[2], preferred_element_ty...  11.1 us
    all_to_all x2, starting transfers between devices, move_rows(): return lax.all_to_all(rows, 'band', split_axis=0, concat_axis=0, tiled=True)  8.91 us
    dot_general x4, matrix products, block_terms(): jnp.einsum('bqhe,bkhe->bhqk', shaped[0], shaped[1], preferred_element_typ...  8.12 us
  transfers between devices with their start and end apart: 14, of which 8 were waited for; matrix products, arithmetic and copies ran while one was open for 11% of the time, Pallas kernels for 0%

profile of v1, /device:TPU:0, one launch (start us, length us, event | category | flops | bytes accessed | tf_op | source)
XLA Modules:
  0.0 201.5 jit_solution(16791798259761796322)
XLA Ops:
  7.2 9.0 %all_gather.12 = bf16[256,1024]{1,0:T(8,128)(2,1)S(1)} all-gather(bf16[256,256]{1,0:T(8,128)(2,1)} %param.11), channel_id=1, replica_groups=mesh['band'=8,'mp'=4] {'mp'}, dimensions={1}, use_global_device_ids=true | all-gather | bytes 655360 | tf_op jit(solution)/shard_map/all_gather | solution.py:60
  16.4 2.1 %fusion.21 = bf16[3,256,256]{2,1,0:T(8,128)(2,1)S(1)} fusion(bf16[3,1024,256]{2,1,0:T(8,128)(2,1)} %param.13, bf16[256,1024]{1,0:T(8,128)(2,1)S(1)} %all_gather.12, f32[1024]{0:T(1024)} %param.12, f32[256]{0:T(256)S(1)} %fusion.61), kind=kOutput, calls=%fused_computation.50 | convolution fusion | flops 403898368 | bytes 2495488 | tf_op jit(solution)/shard_map/jvp(lu,xuh->xlh)/dot_general | solution.py:32
  19.7 1.2 fusion.73
  20.9 0.6 copy-done.25
  21.5 1.2 fusion.29
  22.9 1.1 convolution_convert_fusion.3
  24.3 2.2 %scatter_custom_fusion.1 = bf16[384]{0:T(512)(128)(2,1)S(1)} fusion(s32[256]{0:T(256)S(1)} %bitcast.151, bf16[256]{0:T(256)(128)(2,1)S(1)} %convert_element_type.204, bf16[]{:T(256)} %constant.21.clone.1), kind=kCustom, calls=%fused_computation.136 | custom fusion | bytes 770 | tf_op jit(solution)/shard_map/scatter | solution.py:106
  26.5 0.7 all_to_all.41
  27.1 5.8 %all-to-all-start = ((bf16[8,48,1]{1,2,0:T(2,128)(2,1)}), bf16[8,48,1]{1,2,0:T(2,128)(2,1)S(1)}, u32[]{:S(2)}, u32[]{:S(2)}) async-start(bf16[8,48,1]{1,2,0:T(2,128)(2,1)} %all_to_all.41), calls=%async_computation.1 | async-start | bytes 8192 | tf_op jit(solution)/shard_map/all_to_all | solution.py:113
  33.0 2.5 %scatter_custom_fusion.2 = bf16[384,256]{1,0:T(8,128)(2,1)} fusion(s32[256]{0:T(256)S(1)} %bitcast.152, bf16[256,256]{1,0:T(8,128)(2,1)} %param.21, bf16[]{:T(256)} %constant.21.clone.1), kind=kCustom, calls=%fused_computation.106 | custom fusion | bytes 197120 | tf_op jit(solution)/shard_map/scatter | solution.py:108
  35.4 4.0 %all-to-all-done = bf16[8,48,1]{1,2,0:T(2,128)(2,1)S(1)} async-done(((bf16[8,48,1]{1,2,0:T(2,128)(2,1)}), bf16[8,48,1]{1,2,0:T(2,128)(2,1)S(1)}, u32[]{:S(2)}, u32[]{:S(2)}) %all-to-all-start) | async-done | bytes 800 | tf_op jit(solution)/shard_map/all_to_all | solution.py:113
  39.4 3.4 %all-to-all-start.2 = ((bf16[8,48,256]{2,1,0:T(8,128)(2,1)}), bf16[8,48,256]{2,1,0:T(8,128)(2,1)S(1)}, u32[]{:S(2)}, u32[]{:S(2)}) async-start(bf16[8,48,256]{2,1,0:T(8,128)(2,1)} %bitcast.17), calls=%async_computation.4 | async-start | bytes 393216 | tf_op jit(solution)/shard_map/all_to_all | solution.py:70
  43.0 0.9 fusion.43
  43.9 6.7 %all-to-all-done.2 = bf16[8,48,256]{2,1,0:T(8,128)(2,1)S(1)} async-done(((bf16[8,48,256]{2,1,0:T(8,128)(2,1)}), bf16[8,48,256]{2,1,0:T(8,128)(2,1)S(1)}, u32[]{:S(2)}, u32[]{:S(2)}) %all-to-all-start.2) | async-done | bytes 196640 | tf_op jit(solution)/shard_map/all_to_all | solution.py:70
  50.5 0.7 copy-done.5
  51.2 8.4 %all_gather.14 = bf16[384,1024]{1,0:T(8,128)(2,1)S(1)} all-gather(bf16[384,256]{1,0:T(8,128)(2,1)} %bitcast.133), channel_id=1, replica_groups=mesh['band'=8,'mp'=4] {'mp'}, dimensions={1}, use_global_device_ids=true | all-gather | bytes 983040 | tf_op jit(solution)/shard_map/all_gather | solution.py:60
  59.7 2.5 %scatter_custom_fusion = bf16[384,256]{1,0:T(8,128)(2,1)} fusion(s32[256]{0:T(256)S(1)} %bitcast.153, bf16[256,256]{1,0:T(8,128)(2,1)} %reduce-scatter.5.cloned.1.call-done, bf16[256,256]{1,0:T(8,128)(2,1)S(1)} %copy-done.13, bf16[]{:T(256)} %constant.21.clone.1), kind=kCustom, calls=%fused_computation.101 | custom fusion | flops 262144 | bytes 458754 | tf_op jit(solution)/shard_map/scatter | solution.py:110
  62.2 0.9 constant_dynamic-slice_fusion
  63.1 0.9 collective-permute-start
  64.0 1.1 convolution_convert_fusion.9
  65.1 0.5 collective-permute-start.1
  65.7 2.1 %collective-permute-start.2 = (bf16[48,256]{1,0:T(8,128)(2,1)S(1)}, bf16[48,256]{1,0:T(8,128)(2,1)S(1)}, u32[]{:S(2)}, u32[]{:S(2)}) collective-permute-start(bf16[48,256]{1,0:T(8,128)(2,1)S(1)} %get-tuple-element.14), channel_id=1, source_target_pairs={{0,12},{4,8},{8,4},{12,0},{16,28},{20,24},{24,20},{28,16},{1,13},{... | collective-permute-start | bytes 73736 | tf_op jit(solution)/shard_map/ppermute | solution.py:23
  67.7 0.5 collective-permute-start.3
  68.2 2.8 %collective-permute-start.4 = (bf16[48,256]{1,0:T(8,128)(2,1)S(1)}, bf16[48,256]{1,0:T(8,128)(2,1)S(1)}, u32[]{:S(2)}, u32[]{:S(2)}) collective-permute-start(bf16[48,256]{1,0:T(8,128)(2,1)S(1)} %get-tuple-element.12), channel_id=1, source_target_pairs={{0,20},{4,16},{8,28},{12,24},{16,4},{20,0},{24,12},{28,8},{1,21},{... | collective-permute-start | bytes 73736 | tf_op jit(solution)/shard_map/ppermute | solution.py:23
  71.0 1.1 collective-permute-start.5
  72.1 3.4 %collective-permute-start.6 = (bf16[48,256]{1,0:T(8,128)(2,1)S(1)}, bf16[48,256]{1,0:T(8,128)(2,1)S(1)}, u32[]{:S(2)}, u32[]{:S(2)}) collective-permute-start(bf16[48,256]{1,0:T(8,128)(2,1)S(1)} %get-tuple-element.10), channel_id=1, source_target_pairs={{0,28},{4,24},{8,20},{12,16},{16,12},{20,8},{24,4},{28,0},{1,29},{... | collective-permute-start | bytes 73736 | tf_op jit(solution)/shard_map/ppermute | solution.py:23
  75.5 1.1 collective-permute-done.5
  76.6 2.0 collective-permute-done.6
  78.6 0.7 copy-done.6
  79.3 8.2 %all_gather.13 = bf16[384,1024]{1,0:T(8,128)(2,1)S(1)} all-gather(bf16[384,256]{1,0:T(8,128)(2,1)S(1)} %constant_dynamic-update-slice_fusion.6), channel_id=1, replica_groups=mesh['band'=8,'mp'=4] {'mp'}, dimensions={1}, use_global_device_ids=true | all-gather | bytes 983040 | tf_op jit(solution)/shard_map/all_gather | solution.py:60
  87.7 1.1 fusion.18
  88.8 0.7 fusion.71
  89.6 3.4 %fusion.74 = (f32[4,384]{1,0:T(4,128)S(1)}, f32[4,384,384]{1,2,0:T(8,128)}) fusion(pred[384,384]{0,1:T(8,128)(4,1)} %fusion.43, bf16[384,4,64]{0,2,1:T(8,128)(2,1)} %bitcast.146, bf16[384,4,64]{0,2,1:T(8,128)(2,1)S(1)} %bitcast.143), kind=kOutput, calls=%fused_computation.146 | convolution fusion | flops 77857152 | bytes 2906112 | tf_op jit(solution)/shard_map/jvp()/sub | solution.py:43
  93.0 3.7 %fusion.7 = (f32[4,384]{1,0:T(4,128)S(1)}, bf16[4,384,384]{1,2,0:T(8,128)(2,1)}, bf16[4,384,384]{1,2,0:T(8,128)(2,1)}) fusion(f32[4,384,384]{1,2,0:T(8,128)} %get-tuple-element.21, f32[4,384]{1,0:T(4,128)S(1)} %multiply_divide_fusion, f32[4,384]{1,0:T(4,128)S(1)} %get-tuple-element.20, bf16[4,64,384]{2,1,0:T(8,128)(2,1)S(1)} %bitcast.137, ...), kind=kOutput, calls=%fused_computation.19 | convolution fusion | flops 79624704 | bytes 5130240 | tf_op jit(solution)/shard_map/transpose(jvp(bhqk,bkhe->bqhe))/dot_general | solution.py:46
  96.7 3.9 %fusion.26 = bf16[1,1,384,4,64]{2,4,3,1,0:T(8,128)(2,1)} fusion(bf16[384,4,64]{0,2,1:T(8,128)(2,1)} %bitcast.147, bf16[4,384,384]{1,2,0:T(8,128)(2,1)} %get-tuple-element.22, f32[4,384]{1,0:T(4,128)S(1)} %neg.13, f32[4,384]{1,0:T(4,128)S(1)} %get-tuple-element.20, pred[384,384]{0,1:T(8,128)(4,1)} %fusion.43, bf16[384,4,64]{0,2,1:T(8,128)(2,1)S(1)} %bitcast.144), kind=kOutput, calls=%fused_computation.61 | convolution fusion | flops 156403584 | bytes 1929216 | tf_op jit(solution)/shard_map/transpose(jvp(bqhe,bkhe->bhqk))/dot_general | solution.py:39
  100.7 3.7 %fusion.27 = bf16[1,1,384,4,64]{2,4,3,1,0:T(8,128)(2,1)} fusion(bf16[384,4,64]{0,2,1:T(8,128)(2,1)S(1)} %bitcast.145, bf16[4,384,384]{1,2,0:T(8,128)(2,1)} %get-tuple-element.22, f32[4,384]{1,0:T(4,128)S(1)} %neg.13, f32[4,384]{1,0:T(4,128)S(1)} %get-tuple-element.20, pred[384,384]{0,1:T(8,128)(4,1)} %fusion.43, bf16[384,4,64]{0,2,1:T(8,128)(2,1)S(1)} %bitcast.148), kind=kOutput, calls=%fused_computation.62 | convolution fusion | flops 156403584 | bytes 1929216 | tf_op jit(solution)/shard_map/transpose(jvp(bqhe,bkhe->bhqk))/dot_general | solution.py:39
  104.3 1.8 fusion.28
  106.1 1.1 pad_add_fusion
  107.2 1.1 copy.95
  108.3 2.0 fusion.13
  110.3 1.3 fusion.9
  111.7 23.0 %reduce-scatter.9.cloned.1.call-done = bf16[384,256]{1,0:T(8,128)(2,1)} async-done(((bf16[384,1024]{1,0:T(8,128)(2,1)}), bf16[384,256]{1,0:T(8,128)(2,1)}) %reduce-scatter.9.cloned.1.call-update) | async-done | bytes 196624 | tf_op jit(solution)/shard_map/reduce_scatter | solution.py:64
  134.7 1.8 add_convert_fusion
  136.5 5.5 %all-to-all-start.3 = ((bf16[8,48,256]{2,1,0:T(8,128)(2,1)}), bf16[8,48,256]{2,1,0:T(8,128)(2,1)S(1)}, u32[]{:S(2)}, u32[]{:S(2)}) async-start(bf16[8,48,256]{2,1,0:T(8,128)(2,1)} %bitcast.36), calls=%async_computation.6 | async-start | bytes 393216 | tf_op jit(solution)/shard_map/all_to_all | solution.py:70
  142.1 1.7 convolution_convert_fusion.10
  143.8 1.3 convolution_convert_fusion.1
  145.2 4.8 %all-to-all-done.3 = bf16[8,48,256]{2,1,0:T(8,128)(2,1)S(1)} async-done(((bf16[8,48,256]{2,1,0:T(8,128)(2,1)}), bf16[8,48,256]{2,1,0:T(8,128)(2,1)S(1)}, u32[]{:S(2)}, u32[]{:S(2)}) %all-to-all-start.3) | async-done | bytes 196640 | tf_op jit(solution)/shard_map/all_to_all | solution.py:70
  150.0 1.2 gather_fusion.1
  151.1 6.7 %all-gather = bf16[256,1024]{1,0:T(8,128)(2,1)S(1)} all-gather(bf16[256,256]{1,0:T(8,128)(2,1)S(1)} %gather_fusion.1), channel_id=2, replica_groups=mesh['band'=8,'mp'=4] {'mp'}, dimensions={1}, use_global_device_ids=true | all-gather | bytes 655360 | tf_op jit(solution)/shard_map/all_gather | solution.py:60
  157.9 0.3 convolution_convert_fusion.14
  158.4 1.3 multiply_reduce_fusion
  159.7 1.4 fusion.30
  161.1 0.2 fusion.32
  161.4 0.3 fusion.31
  161.8 0.4 copy.105
  162.2 0.3 reshape.260
  162.5 2.1 %fusion.37 = (f32[256]{0:T(256)S(1)}, f32[256,1024]{1,0:T(8,128)S(1)}) fusion(bf16[256,1024]{1,0:T(8,128)(2,1)S(1)} %all_gather.12, f32[1024]{0:T(1024)S(1)} %copy-done.23, bf16[3,1024,256]{2,1,0:T(8,128)(2,1)} %param.13, bf16[3,256,256]{1,2,0:T(8,128)(2,1)S(1)} %reshape.260), kind=kOutput, calls=%fused_computation.77 | convolution fusion | flops 404225792 | bytes 3544064 | tf_op jit(solution)/shard_map/transpose(jvp(lu,xuh->xlh))/dot_general | solution.py:32
  164.6 1.1 fusion.33
  165.7 3.5 %reduce-scatter.7.cloned.1.call-done = bf16[384,256]{1,0:T(8,128)(2,1)} async-done(((bf16[384,1024]{1,0:T(8,128)(2,1)}), bf16[384,256]{1,0:T(8,128)(2,1)}) %reduce-scatter.7.cloned.1.call-update) | async-done | bytes 196624 | tf_op jit(solution)/shard_map/reduce_scatter | solution.py:64
  169.2 1.0 add_convert_fusion.1
  170.2 13.3 %all_to_all.46 = bf16[8,48,256]{2,1,0:T(8,128)(2,1)S(1)} all-to-all(bf16[8,48,256]{2,1,0:T(8,128)(2,1)S(1)} %bitcast.136), channel_id=1, replica_groups=mesh['band'=8,'mp'=4] {'band'}, dimensions={0} | all-to-all | bytes 393216 | tf_op jit(solution)/shard_map/all_to_all | solution.py:70
  183.4 1.8 gather_fusion
  185.2 8.2 %reduce-scatter.11.cloned.1.call-done = bf16[256,256]{1,0:T(8,128)(2,1)} async-done(((bf16[256,1024]{1,0:T(8,128)(2,1)}), bf16[256,256]{1,0:T(8,128)(2,1)}) %reduce-scatter.11.cloned.1.call-update) | async-done | bytes 131088 | tf_op jit(solution)/shard_map/reduce_scatter | solution.py:64
  193.4 1.6 add_convert_fusion.2
  (104 shorter events, 2.6 us)
Async XLA Ops:
  7.2 80.5 %copy-start = (bf16[3,1024,256]{2,1,0:T(8,128)(2,1)S(1)}, bf16[3,1024,256]{2,1,0:T(8,128)(2,1)}, u32[]{:S(2)}) copy-start(bf16[3,1024,256]{2,1,0:T(8,128)(2,1)} %param.16) | copy-start | bytes 4718596
  7.2 52.5 %reduce-scatter.5.cloned.1.call-start = ((), (), s32[]{:S(2)}) async-start(), calls=%async_computation.8 | async-start | bytes 655360 | tf_op jit(solution)/shard_map/reduce_scatter | solution.py:64
  16.4 2.8 %copy-start.24 = (s32[256]{0:T(256)S(1)}, s32[256]{0:T(256)}, u32[]{:S(2)}) copy-start(s32[256]{0:T(256)} %param.18) | copy-start | bytes 3076
  18.8 4.1 %copy-start.15 = (bf16[2,128,4,64]{1,3,2,0:T(8,128)(2,1)}, bf16[2,128,4,64]{1,3,2,0:T(8,128)(2,1)S(1)}, u32[]{:S(2)}) copy-start(bf16[2,128,4,64]{1,3,2,0:T(8,128)(2,1)S(1)} %copy.84) | copy-start | bytes 393220
  19.0 3.9 %copy-start.3 = (bf16[256,1024]{1,0:T(8,128)(2,1)S(1)}, bf16[256,1024]{1,0:T(8,128)(2,1)}, u32[]{:S(2)}) copy-start(bf16[256,1024]{1,0:T(8,128)(2,1)} %param.14) | copy-start | bytes 1572868
  19.2 3.5 %copy-start.17 = (bf16[2,128,4,64]{1,3,2,0:T(8,128)(2,1)}, bf16[2,128,4,64]{1,3,2,0:T(8,128)(2,1)S(1)}, u32[]{:S(2)}) copy-start(bf16[2,128,4,64]{1,3,2,0:T(8,128)(2,1)S(1)} %copy.85) | copy-start | bytes 393220
  19.3 1.6 copy-start.19
  19.6 3.1 %copy-start.10 = (bf16[2,128,4,64]{1,3,2,0:T(8,128)(2,1)}, bf16[2,128,4,64]{1,3,2,0:T(8,128)(2,1)S(1)}, u32[]{:S(2)}) copy-start(bf16[2,128,4,64]{1,3,2,0:T(8,128)(2,1)S(1)} %copy.86) | copy-start | bytes 393220
  19.6 4.4 %copy-start.27 = (s32[256]{0:T(256)S(1)}, s32[256]{0:T(256)}, u32[]{:S(2)}) copy-start(s32[256]{0:T(256)} %param.20) | copy-start | bytes 3076
  19.7 4.4 %copy-start.21 = (s32[256,1]{0,1:T(1,128)S(1)}, s32[256,1]{0,1:T(1,128)}, u32[]{:S(2)}) copy-start(s32[256,1]{0,1:T(1,128)} %param.19) | copy-start | bytes 3076
  20.9 0.6 copy-start.25
  22.7 36.9 %copy-start.13 = (bf16[256,256]{1,0:T(8,128)(2,1)S(1)}, bf16[256,256]{1,0:T(8,128)(2,1)}, u32[]{:S(2)}) copy-start(bf16[256,256]{1,0:T(8,128)(2,1)} %param.11) | copy-start | bytes 393220
  22.9 41.1 %copy-start.1 = (bf16[256,1024]{1,0:T(8,128)(2,1)S(1)}, bf16[256,1024]{1,0:T(8,128)(2,1)}, u32[]{:S(2)}) copy-start(bf16[256,1024]{1,0:T(8,128)(2,1)} %param.17) | copy-start | bytes 1572868
  27.1 12.3 %all-to-all-start = ((bf16[8,48,1]{1,2,0:T(2,128)(2,1)}), bf16[8,48,1]{1,2,0:T(2,128)(2,1)S(1)}, u32[]{:S(2)}, u32[]{:S(2)}) async-start(bf16[8,48,1]{1,2,0:T(2,128)(2,1)} %all_to_all.41), calls=%async_computation.1 | async-start | bytes 8192 | tf_op jit(solution)/shard_map/all_to_all | solution.py:113
  39.4 11.1 %all-to-all-start.2 = ((bf16[8,48,256]{2,1,0:T(8,128)(2,1)}), bf16[8,48,256]{2,1,0:T(8,128)(2,1)S(1)}, u32[]{:S(2)}, u32[]{:S(2)}) async-start(bf16[8,48,256]{2,1,0:T(8,128)(2,1)} %bitcast.17), calls=%async_computation.4 | async-start | bytes 393216 | tf_op jit(solution)/shard_map/all_to_all | solution.py:70
  42.8 91.9 %reduce-scatter.9.cloned.1.call-start = ((), (), s32[]{:S(2)}) async-start(), calls=%async_computation.10 | async-start | bytes 983040 | tf_op jit(solution)/shard_map/reduce_scatter | solution.py:64
  50.5 0.7 copy-start.5
  59.6 28.1 %copy-start.22 = (f32[1024]{0:T(1024)S(1)}, f32[1024]{0:T(1024)}, u32[]{:S(2)}) copy-start(f32[1024]{0:T(1024)} %param.15) | copy-start | bytes 12292
  63.1 7.9 %collective-permute-start = (bf16[48,256]{1,0:T(8,128)(2,1)S(1)}, bf16[48,256]{1,0:T(8,128)(2,1)S(1)}, u32[]{:S(2)}, u32[]{:S(2)}) collective-permute-start(bf16[48,256]{1,0:T(8,128)(2,1)S(1)} %get-tuple-element.16), channel_id=1, source_target_pairs={{0,4},{4,0},{8,12},{12,8},{16,20},{20,16},{24,28},{28,24},{1,5},{5... | collective-permute-start | bytes 73736 | tf_op jit(solution)/shard_map/ppermute | solution.py:23
  65.1 6.9 %collective-permute-start.1 = (bf16[48,256]{1,0:T(8,128)(2,1)S(1)}, bf16[48,256]{1,0:T(8,128)(2,1)S(1)}, u32[]{:S(2)}, u32[]{:S(2)}) collective-permute-start(bf16[48,256]{1,0:T(8,128)(2,1)S(1)} %get-tuple-element.15), channel_id=1, source_target_pairs={{0,8},{4,12},{8,0},{12,4},{16,24},{20,28},{24,16},{28,20},{1,9},{5... | collective-permute-start | bytes 73736 | tf_op jit(solution)/shard_map/ppermute | solution.py:23
  65.7 9.8 %collective-permute-start.2 = (bf16[48,256]{1,0:T(8,128)(2,1)S(1)}, bf16[48,256]{1,0:T(8,128)(2,1)S(1)}, u32[]{:S(2)}, u32[]{:S(2)}) collective-permute-start(bf16[48,256]{1,0:T(8,128)(2,1)S(1)} %get-tuple-element.14), channel_id=1, source_target_pairs={{0,12},{4,8},{8,4},{12,0},{16,28},{20,24},{24,20},{28,16},{1,13},{... | collective-permute-start | bytes 73736 | tf_op jit(solution)/shard_map/ppermute | solution.py:23
  67.7 7.7 %collective-permute-start.3 = (bf16[48,256]{1,0:T(8,128)(2,1)S(1)}, bf16[48,256]{1,0:T(8,128)(2,1)S(1)}, u32[]{:S(2)}, u32[]{:S(2)}) collective-permute-start(bf16[48,256]{1,0:T(8,128)(2,1)S(1)} %get-tuple-element.13), channel_id=1, source_target_pairs={{0,16},{4,20},{8,24},{12,28},{16,0},{20,4},{24,8},{28,12},{1,17},{... | collective-permute-start | bytes 73736 | tf_op jit(solution)/shard_map/ppermute | solution.py:23
  68.2 7.2 %collective-permute-start.4 = (bf16[48,256]{1,0:T(8,128)(2,1)S(1)}, bf16[48,256]{1,0:T(8,128)(2,1)S(1)}, u32[]{:S(2)}, u32[]{:S(2)}) collective-permute-start(bf16[48,256]{1,0:T(8,128)(2,1)S(1)} %get-tuple-element.12), channel_id=1, source_target_pairs={{0,20},{4,16},{8,28},{12,24},{16,4},{20,0},{24,12},{28,8},{1,21},{... | collective-permute-start | bytes 73736 | tf_op jit(solution)/shard_map/ppermute | solution.py:23
  71.0 5.6 %collective-permute-start.5 = (bf16[48,256]{1,0:T(8,128)(2,1)S(1)}, bf16[48,256]{1,0:T(8,128)(2,1)S(1)}, u32[]{:S(2)}, u32[]{:S(2)}) collective-permute-start(bf16[48,256]{1,0:T(8,128)(2,1)S(1)} %get-tuple-element.11), channel_id=1, source_target_pairs={{0,24},{4,28},{8,16},{12,20},{16,8},{20,12},{24,0},{28,4},{1,25},{... | collective-permute-start | bytes 73736 | tf_op jit(solution)/shard_map/ppermute | solution.py:23
  72.1 6.5 %collective-permute-start.6 = (bf16[48,256]{1,0:T(8,128)(2,1)S(1)}, bf16[48,256]{1,0:T(8,128)(2,1)S(1)}, u32[]{:S(2)}, u32[]{:S(2)}) collective-permute-start(bf16[48,256]{1,0:T(8,128)(2,1)S(1)} %get-tuple-element.10), channel_id=1, source_target_pairs={{0,28},{4,24},{8,20},{12,16},{16,12},{20,8},{24,4},{28,0},{1,29},{... | collective-permute-start | bytes 73736 | tf_op jit(solution)/shard_map/ppermute | solution.py:23
  78.6 0.7 copy-start.6
  89.6 7.2 %copy-start.8 = (bf16[1,384,256]{1,2,0:T(8,128)(2,1)}, bf16[1,384,256]{1,2,0:T(8,128)(2,1)S(1)}, u32[]{:S(2)}) copy-start(bf16[1,384,256]{1,2,0:T(8,128)(2,1)S(1)} %get-tuple-element.6) | copy-start | bytes 589828
  89.6 3.5 %copy-start.9 = (bf16[384,256]{0,1:T(8,128)(2,1)S(1)}, bf16[384,256]{0,1:T(8,128)(2,1)}, u32[]{:S(2)}) copy-start(bf16[384,256]{0,1:T(8,128)(2,1)} %convolution_convert_fusion.9) | copy-start | bytes 589828
  96.7 3.9 %copy-start.14 = (bf16[1,384,256]{1,2,0:T(8,128)(2,1)S(1)}, bf16[1,384,256]{1,2,0:T(8,128)(2,1)}, u32[]{:S(2)}) copy-start(bf16[1,384,256]{1,2,0:T(8,128)(2,1)} %get-tuple-element.5) | copy-start | bytes 589828
  110.3 1.4 copy-start.26
  110.3 33.5 %copy-start.2 = (bf16[256,1024]{1,0:T(8,128)(2,1)S(1)}, bf16[256,1024]{1,0:T(8,128)(2,1)}, u32[]{:S(2)}) copy-start(bf16[256,1024]{1,0:T(8,128)(2,1)} %param.17) | copy-start | bytes 1572868
  136.5 13.5 %all-to-all-start.3 = ((bf16[8,48,256]{2,1,0:T(8,128)(2,1)}), bf16[8,48,256]{2,1,0:T(8,128)(2,1)S(1)}, u32[]{:S(2)}, u32[]{:S(2)}) async-start(bf16[8,48,256]{2,1,0:T(8,128)(2,1)} %bitcast.36), calls=%async_computation.6 | async-start | bytes 393216 | tf_op jit(solution)/shard_map/all_to_all | solution.py:70
  142.0 27.2 %reduce-scatter.7.cloned.1.call-start = ((), (), s32[]{:S(2)}) async-start(), calls=%async_computation.9 | async-start | bytes 983040 | tf_op jit(solution)/shard_map/reduce_scatter | solution.py:64
  143.8 14.1 %copy-start.4 = (bf16[256,1024]{1,0:T(8,128)(2,1)S(1)}, bf16[256,1024]{1,0:T(8,128)(2,1)}, u32[]{:S(2)}) copy-start(bf16[256,1024]{1,0:T(8,128)(2,1)} %param.14) | copy-start | bytes 1572868
  145.1 13.3 %copy-start.11 = (bf16[2,128,4,64]{1,3,2,0:T(8,128)(2,1)S(1)}, bf16[2,128,4,64]{1,3,2,0:T(8,128)(2,1)}, u32[]{:S(2)}) copy-start(bf16[2,128,4,64]{1,3,2,0:T(8,128)(2,1)} %copy-done.10) | copy-start | bytes 393220
  145.1 48.3 %reduce-scatter.11.cloned.1.call-start = ((), (), s32[]{:S(2)}) async-start(), calls=%async_computation.11 | async-start | bytes 655360 | tf_op jit(solution)/shard_map/reduce_scatter | solution.py:64
  157.9 3.2 %copy-start.18 = (bf16[2,128,4,64]{1,3,2,0:T(8,128)(2,1)S(1)}, bf16[2,128,4,64]{1,3,2,0:T(8,128)(2,1)}, u32[]{:S(2)}) copy-start(bf16[2,128,4,64]{1,3,2,0:T(8,128)(2,1)} %copy-done.17) | copy-start | bytes 393220
  157.9 3.3 %copy-start.20 = (pred[2,128,128]{1,2,0:T(8,128)(4,1)S(1)}, pred[2,128,128]{1,2,0:T(8,128)(4,1)}, u32[]{:S(2)}) copy-start(pred[2,128,128]{1,2,0:T(8,128)(4,1)} %copy-done.19) | copy-start | bytes 98308
  158.2 2.9 %copy-start.12 = (f32[2,4,128,128]{2,3,1,0:T(8,128)S(1)}, f32[2,4,128,128]{2,3,1,0:T(8,128)}, u32[]{:S(2)}) copy-start(f32[2,4,128,128]{2,3,1,0:T(8,128)} %get-tuple-element.19) | copy-start | bytes 1572868
  159.7 1.7 copy-start.16
  161.4 1.0 copy-start.23
  162.4 6.7 %copy-start.7 = (bf16[384,256]{1,0:T(8,128)(2,1)S(1)}, bf16[384,256]{1,0:T(8,128)(2,1)}, u32[]{:S(2)}) copy-start(bf16[384,256]{1,0:T(8,128)(2,1)} %copy-done.6) | copy-start | bytes 589828
Sparse Core Ops, SparseCore 0:
  24.2 22.5 reduce-scatter.4
  111.8 22.9 reduce-scatter.8
  145.4 23.7 reduce-scatter.6
  171.7 21.6 reduce-scatter.10
